TPU v7x, 256 devices: a whole 4x4x8 slice. The times are simulated.
256 devices in a mesh: fsdp: 32 (over x, z_lo, core), tp: 8 (over z_hi, y).
Axes of the slice: x: 4, y: 4, z: 8 (z_hi: 2, z_lo: 4; z = z_hi * 4 + z_lo), core: 2. Of those that a mesh axis runs over, the one named last changes fastest.
Arguments:
- grad_part: float32 [32, 4, 512, 8192], P('fsdp', None, None, 'tp'), may hold values from -6 to 6
- block_of_slot: int32 [64], replicated, may hold values from 0 to 63, each once
- stat_left: float32 [64, 512, 512], P('fsdp', 'tp'), may hold values from -6 to 6
- stat_right: float32 [64, 512, 512], P('fsdp', 'tp'), may hold values from -6 to 6
- basis_left: float32 [64, 512, 512], P('fsdp', 'tp'), may hold values from -0.25 to 0.25
- basis_right: float32 [64, 512, 512], P('fsdp', 'tp'), may hold values from -0.25 to 0.25
- moment: float32 [64, 512, 512], P('fsdp', 'tp'), may hold values from -4 to 4
- second: float32 [64, 512, 512], P('fsdp', 'tp'), may hold values from 0.05 to 2
Outputs:
- update: bfloat16 [4, 512, 8192], P(None, 'fsdp', 'tp')
- new_left: float32 [64, 512, 512], P('fsdp', 'tp')
- new_right: float32 [64, 512, 512], P('fsdp', 'tp')
- new_moment: float32 [64, 512, 512], P('fsdp', 'tp')
- new_second: float32 [64, 512, 512], P('fsdp', 'tp')
Inputs may be any that keep to these rules, and one draw needn't show every extreme that they name: Slot s, held by fsdp index s // 2, carries the state of block block_of_slot[s]; every block has exactly one slot.
All inputs are finite; a program needn't handle non-finite values.
Results may differ from a plain program's by a relative error of at most 0.001.
Values may be sent and summed in bfloat16 or wider, within the bound.
A program may use at most 128 MiB of HBM per device.

v0:
```python
import jax
import jax.numpy as jnp
from jax import lax
from jax.sharding import PartitionSpec as P

first_decay = 0.9
second_decay = 0.95
epsilon = 1e-08
highest = lax.Precision.HIGHEST


def product(form, left, right):
    return jnp.einsum(form, left, right, precision=highest, preferred_element_type=jnp.float32)


def local(grad_part, block_of_slot, stat_left, stat_right, basis_left, basis_right, moment, second):
    panels = grad_part.shape[1]
    local_cols = grad_part.shape[3]
    slab = stat_left.shape[1]
    col_blocks = local_cols // slab
    blocks_total = panels * col_blocks
    summed = lax.psum_scatter(grad_part[0], "fsdp", scatter_dimension=1, tiled=True)
    row_piece = summed.shape[1]
    by_block = jnp.transpose(
        summed.reshape(panels, row_piece, col_blocks, slab), (0, 2, 3, 1)
    ).reshape(blocks_total, slab, row_piece)
    by_slot = jnp.take(by_block, block_of_slot, axis=0)
    column_part = lax.all_to_all(by_slot, "fsdp", split_axis=0, concat_axis=2, tiled=True)
    grad_cols = lax.all_gather(column_part, "tp", axis=1, tiled=True)
    left_rows = lax.all_gather(basis_left, "tp", axis=1, tiled=True)
    column_index = lax.axis_index("tp")
    row_slab = lax.dynamic_slice_in_dim(grad_cols, column_index * slab, slab, 2)
    new_left = second_decay * stat_left + (1.0 - second_decay) * product(
        "bki,bkj->bij", row_slab, grad_cols
    )
    new_right = second_decay * stat_right + (1.0 - second_decay) * product(
        "bik,bjk->bij", column_part, grad_cols
    )
    partial_rot = product("bik,bkj->bij", basis_right, grad_cols)
    rotated = product("bir,bmr->bim", partial_rot, left_rows)
    new_moment = first_decay * moment + (1.0 - first_decay) * rotated
    new_second = second_decay * second + (1.0 - second_decay) * rotated * rotated
    direction = new_moment / (jnp.sqrt(new_second) + epsilon)
    half_back = product("bkr,brm->bkm", direction, left_rows)
    returned = lax.psum_scatter(
        product("bki,bkm->ibm", basis_right, half_back), "tp", scatter_dimension=0, tiled=True
    )
    update_cols = jnp.transpose(returned, (1, 0, 2)).astype(jnp.bfloat16)
    by_source = lax.all_to_all(update_cols, "fsdp", split_axis=2, concat_axis=0, tiled=True)
    inverse = (
        jnp.zeros((blocks_total,), jnp.int32)
        .at[block_of_slot]
        .set(jnp.arange(blocks_total, dtype=jnp.int32))
    )
    block_order = jnp.take(by_source, inverse, axis=0)
    out_rows = by_source.shape[2]
    update = jnp.transpose(
        block_order.reshape(panels, col_blocks, slab, out_rows), (0, 3, 1, 2)
    ).reshape(panels, out_rows, local_cols)
    return (update, new_left, new_right, new_moment, new_second)


def solution(mesh):
    return jax.shard_map(
        local,
        mesh=mesh,
        in_specs=(
            P("fsdp", None, None, "tp"),
            P(),
            P("fsdp", "tp", None),
            P("fsdp", "tp", None),
            P("fsdp", "tp", None),
            P("fsdp", "tp", None),
            P("fsdp", "tp", None),
            P("fsdp", "tp", None),
        ),
        out_specs=(
            P(None, "fsdp", "tp"),
            P("fsdp", "tp", None),
            P("fsdp", "tp", None),
            P("fsdp", "tp", None),
            P("fsdp", "tp", None),
        ),
        check_vma=False,
    )
```

profile of v0, /device:TPU:1, one launch (start us, length us, event | category | flops | bytes accessed | tf_op | source)
XLA Modules:
  0.0 501.9 jit_solution(4868439695616293349)
XLA Ops:
  7.2 0.0 copy-start
  7.2 0.0 reduce-scatter.2.cloned.1.call-start
  7.2 0.0 copy-start.9
  7.2 0.7 reduce-scatter.2.cloned.1.call-update
  7.9 0.0 all-gather.3.cloned.1.call-start
  8.0 164.7 %reduce-scatter.2.cloned.1.call-done = f32[4,16,1024]{2,1,0:T(8,128)} async-done(((f32[4,512,1024]{2,1,0:T(8,128)}), f32[4,16,1024]{2,1,0:T(8,128)}) %reduce-scatter.2.cloned.1.call-update) | async-done | bytes 262160 | tf_op jit(solution)/shard_map/reduce_scatter | solution.py:22
  172.8 1.1 reshape.33
  173.8 0.2 copy.34
  174.0 0.6 gather_fusion
  174.7 0.1 fusion.14
  174.8 0.3 reshape.66
  175.1 0.0 copy-start.10
  175.1 19.1 %all_to_all.36 = f32[32,1,2048]{2,1,0:T(1,128)S(1)} all-to-all(f32[32,1,2048]{2,1,0:T(1,128)S(1)} %reshape.66), channel_id=1, replica_groups=mesh['fsdp'=32,'tp'=8] {'fsdp'}, dimensions={0} | all-to-all | bytes 524288 | tf_op jit(solution)/shard_map/all_to_all | solution.py:28
  194.3 0.5 broadcast.43
  194.8 1.3 reduce
  196.0 0.2 reshape.67
  196.3 0.0 copy-start.6
  196.3 0.0 copy-start.7
  196.3 0.9 copy.36
  197.2 0.0 all-gather.3.cloned.1.call-update
  197.2 0.0 all-gather.5.cloned.1.call-start
  197.3 0.7 all-gather.5.cloned.1.call-update
  198.0 0.8 scatter_custom_fusion
  198.8 0.1 broadcast_in_dim.28
  198.9 0.6 dynamic-slice
  200.2 69.4 %all-gather.3.cloned.1.call-done = f32[2,512,512]{2,1,0:T(8,128)} async-done(((f32[2,64,512]{2,1,0:T(8,128)}), f32[2,512,512]{2,1,0:T(8,128)}) %all-gather.3.cloned.1.call-update) | async-done | bytes 2097168 | tf_op jit(solution)/shard_map/all_gather | solution.py:29
  269.5 3.0 fusion.15
  272.6 71.4 %all-gather.5.cloned.1.call-done = f32[2,512,512]{2,1,0:T(8,128)} async-done(((f32[2,64,512]{2,1,0:T(8,128)}), f32[2,512,512]{2,1,0:T(8,128)}) %all-gather.5.cloned.1.call-update) | async-done | bytes 2097168 | tf_op jit(solution)/shard_map/all_gather | solution.py:30
  343.9 3.9 fusion.3
  347.8 0.0 copy-start.4
  347.8 0.0 copy-start.3
  347.8 0.7 copy-done.4
  348.5 1.5 fusion.4
  350.0 1.8 convolution_bitcast_fusion
  351.8 2.4 copy.37
  354.3 109.1 %all-reduce.2 = bf16[512,2,512]{2,1,0:T(2,128)(2,1)} all-reduce(f32[512,2,512]{2,1,0:T(2,128)} %copy.37), channel_id=3, replica_groups=mesh['fsdp'=32,'tp'=8] {'tp'}, use_global_device_ids=true, to_apply=%region_2.3.clone | all-reduce | flops 524288 | bytes 3145728
  463.4 1.0 fusion.8
  464.3 0.2 copy.38
  464.5 0.8 reshape.68
  465.4 19.3 %all-to-all-start.1 = ((bf16[32,2,1024]{2,1,0:T(2,128)(2,1)}), bf16[32,2,1024]{2,1,0:T(2,128)(2,1)S(1)}, u32[]{:S(2)}, u32[]{:S(2)}) async-start(bf16[32,2,1024]{2,1,0:T(2,128)(2,1)} %reshape.68), calls=%async_computation.2 | async-start | bytes 262144 | tf_op jit(solution)/shard_map/all_to_all | solution.py:49
  484.7 2.9 fusion
  487.6 2.1 fusion.1
  489.7 3.6 all-to-all-done.1
  493.4 0.2 reshape.69
  493.7 0.6 gather_fusion.1
  494.3 0.1 select_bitcast_fusion
  494.5 0.1 copy.41
  494.5 0.9 reshape.35
  (24 shorter events, 0.2 us)
Async XLA Ops:
  7.2 262.4 %copy-start = (f32[2,64,512]{2,1,0:T(8,128)S(1)}, f32[2,64,512]{2,1,0:T(8,128)}, u32[]{:S(2)}) copy-start(f32[2,64,512]{2,1,0:T(8,128)} %param.13) | copy-start | bytes 786436
  7.2 165.6 %reduce-scatter.2.cloned.1.call-start = ((), (), s32[]{:S(2)}) async-start(), calls=%async_computation.3 | async-start | bytes 8650752 | tf_op jit(solution)/shard_map/reduce_scatter | solution.py:22
  7.2 0.7 copy-start.9
  7.9 261.6 %all-gather.3.cloned.1.call-start = ((), (), s32[]{:S(2)}) async-start(), calls=%async_computation.4 | async-start | bytes 2359296 | tf_op jit(solution)/shard_map/all_gather | solution.py:29
  175.1 23.8 %copy-start.10 = (u32[256]{0:T(256)S(1)}, u32[256]{0:T(256)}, u32[]{:S(2)}) copy-start(u32[256]{0:T(256)} %constant.58) | copy-start | bytes 3076
  196.3 147.6 %copy-start.6 = (f32[2,64,512]{2,1,0:T(8,128)S(1)}, f32[2,64,512]{2,1,0:T(8,128)}, u32[]{:S(2)}) copy-start(f32[2,64,512]{2,1,0:T(8,128)} %param.15) | copy-start | bytes 786436
  196.3 147.6 %copy-start.7 = (f32[2,64,512]{2,1,0:T(8,128)S(1)}, f32[2,64,512]{2,1,0:T(8,128)}, u32[]{:S(2)}) copy-start(f32[2,64,512]{2,1,0:T(8,128)} %param.14) | copy-start | bytes 786436
  197.2 146.7 %all-gather.5.cloned.1.call-start = ((), (), s32[]{:S(2)}) async-start(), calls=%async_computation.5 | async-start | bytes 2359296 | tf_op jit(solution)/shard_map/all_gather | solution.py:30
  343.9 4.6 copy-start.2
  347.8 0.7 copy-start.4
  347.8 4.0 copy-start.3
  354.3 130.4 %copy-start.1 = (f32[2,512,512]{2,1,0:T(8,128)S(1)}, f32[2,512,512]{2,1,0:T(8,128)}, u32[]{:S(2)}) copy-start(f32[2,512,512]{2,1,0:T(8,128)} %all-gather.3.cloned.1.call-done) | copy-start | bytes 6291460
  354.3 130.4 %copy-start.5 = (f32[2,64,512]{2,1,0:T(8,128)S(1)}, f32[2,64,512]{2,1,0:T(8,128)}, u32[]{:S(2)}) copy-start(f32[2,64,512]{2,1,0:T(8,128)} %param.11) | copy-start | bytes 786436
  465.4 22.2 %copy-start.8 = (f32[2,64,512]{2,1,0:T(8,128)S(1)}, f32[2,64,512]{2,1,0:T(8,128)}, u32[]{:S(2)}) copy-start(f32[2,64,512]{2,1,0:T(8,128)} %param.10) | copy-start | bytes 786436
  465.4 28.0 %all-to-all-start.1 = ((bf16[32,2,1024]{2,1,0:T(2,128)(2,1)}), bf16[32,2,1024]{2,1,0:T(2,128)(2,1)S(1)}, u32[]{:S(2)}, u32[]{:S(2)}) async-start(bf16[32,2,1024]{2,1,0:T(2,128)(2,1)} %reshape.68), calls=%async_computation.2 | async-start | bytes 262144 | tf_op jit(solution)/shard_map/all_to_all | solution.py:49
Sparse Core Ops, SparseCore 0:
  10.6 162.1 reduce-scatter.1
  197.4 72.1 all-gather.2
  272.2 71.7 all-gather.4
where the time goes:
time: 502 us
  waiting for transfers between devices  310 us (62%)
  blocking collectives  128 us (25%)
  starting transfers between devices  19.4 us (4%)
  matrix products  15.3 us (3%)
  between operations  14.7 us (3%)
  local copies, waits for them, and re-layouts  12.4 us (2%)
    reduce_scatter x1, waiting for transfers between devices, local(): lax.psum_scatter(grad_part[0], 'fsdp', scatter_dimension=1, tiled=True)  165 us
    unnamed x1, blocking collectives  109 us
    all_gather x1, waiting for transfers between devices, local(): left_rows = lax.all_gather(basis_left, 'tp', axis=1, tiled=True)  71.4 us
    all_gather x1, waiting for transfers between devices, local(): grad_cols = lax.all_gather(column_part, 'tp', axis=1, tiled=True)  69.4 us
    all_to_all x1, starting transfers between devices, local(): lax.all_to_all(update_cols, 'fsdp', split_axis=2, concat_axis=0, tiled=True)  19.3 us
    all_to_all x1, blocking collectives, local(): lax.all_to_all(by_slot, 'fsdp', split_axis=0, concat_axis=2, tiled=True)  19.1 us
    dot_general x6, matrix products, product(): jnp.einsum(form, left, right, precision=highest, preferred_element_type=j...  15.3 us
  transfers between devices with their start and end apart: 4, of which 4 were waited for; matrix products, arithmetic and copies ran while one was open for 2% of the time, Pallas kernels for 0%

commit v1 on v0

v1 whole, which is shorter than its diff:
```python
import jax
import jax.numpy as jnp
from jax import lax
from jax.experimental import pallas as pl
from jax.experimental.pallas import tpu as pltpu
from jax.sharding import PartitionSpec as P

first_decay = 0.9
second_decay = 0.95
epsilon = 1e-08
MESH = pl.DeviceIdType.MESH
f32, bf16, i16, i32 = jnp.float32, jnp.bfloat16, jnp.int16, jnp.int32
FAR = (2, 1, 3)


def roll_half(v):
    return pltpu.roll(v, 64, 1)


def lane_iota(rows):
    return lax.broadcasted_iota(i32, (rows, 128), 1)


def split(v):
    high = v.astype(bf16)
    return high, (v - high.astype(f32)).astype(bf16)


def dot(a, b, dims):
    return lax.dot_general(a, b, (dims, ((), ())), preferred_element_type=f32)


PLAIN = ((1,), (0,))
MINOR = ((1,), (1,))


def dot3(a, bh, bl, dims):
    ah, al = split(a)
    return dot(ah, bh, dims) + (dot(ah, bl, dims) + dot(al, bh, dims))


def encode(v, ref):
    top = jnp.max(jnp.abs(v), axis=0, keepdims=True)
    power = jnp.ceil(jnp.log2(jnp.maximum(top, 1e-30) * (1.0 / 32500.0)))
    ref[pl.ds(0, 256), :] = jnp.round(v * jnp.exp2(-power)).astype(i32).astype(i16)
    ref[pl.ds(256, 16), :] = jnp.broadcast_to(power, (16, 128)).astype(i32).astype(i16)


def scale_of(ref):
    return jnp.exp2(ref[pl.ds(256, 16), :].astype(i32).astype(f32))[0:1]


def decode(ref):
    return ref[pl.ds(0, 256), :].astype(i32).astype(f32) * scale_of(ref)


def kernel(
    bos, inv, grad_h, sl_h, sr_h, bl_h, br_h, mo_h, se_h,
    upd_h, nl_h, nr_h, nm_h, ns_h,
    g, sl, sr, bl, br, mo, se, upd,
    cs, cr, xs, xr, zs, zr, za, gslab, ag, ah, left, rmsg, rc, rct, gt, hb, tmp, bk, a2s, a2r,
    loc, g_sem, out_sem, c_s, c_r, x_s, x_r, z_s, z_r, l_s, l_r, r_s, r_r, g_s, g_r, h_s, h_r, a_s, a_r,
):
    f = lax.axis_index("fsdp")
    t = lax.axis_index("tp")
    x, zl, c = f // 8, (f // 2) % 4, f % 2
    zh, y = t // 4, t % 4

    def fdev(x_, z_, c_):
        return ((x_ * 4 + z_) * 2 + c_, t)

    def tdev(zh_, y_):
        return (f, zh_ * 4 + y_)

    def remote(src, dst, ss, rs, dev):
        return pltpu.make_async_remote_copy(
            src_ref=src, dst_ref=dst, send_sem=ss, recv_sem=rs, device_id=dev, device_id_type=MESH
        )

    loads = [
        pltpu.make_async_copy(src, dst, loc.at[i])
        for i, (src, dst) in enumerate(((bl_h, bl), (br_h, br), (sl_h, sl), (sr_h, sr), (mo_h, mo), (se_h, se)))
    ]

    def grad_load(i):
        p, u = i // 8, i % 8
        return pltpu.make_async_copy(
            grad_h.at[p, :, :, pl.ds(pl.multiple_of(u * 128, 128), 128)], g.at[pl.ds(2 * i, 2)], g_sem.at[i]
        )

    loads[0].start()
    loads[1].start()

    @pl.loop(0, 32)
    def _(i):
        grad_load(i).start()

    for cp in loads[2:]:
        cp.start()

    barrier = pltpu.get_barrier_semaphore()

    @pl.loop(1, 32)
    def _(d):
        pl.semaphore_signal(barrier, inc=1, device_id=((f + d) % 32, t), device_id_type=MESH)

    @pl.loop(1, 8)
    def _(d):
        pl.semaphore_signal(barrier, inc=1, device_id=(f, (t + d) % 8), device_id_type=MESH)

    def core_copy(s, dx):
        return remote(cs.at[s, dx], cr.at[s, dx], c_s.at[s, dx], c_r.at[s, dx], fdev(x, zl, 1 - c))

    def x_copy(s, dx, z):
        return remote(
            xs.at[s, dx - 1, z], xr.at[s, dx - 1, z], x_s.at[s, dx - 1, z], x_r.at[s, dx - 1, z],
            fdev((x + dx) % 4, zl, c),
        )

    def z_copy(s, dz):
        return remote(
            zs.at[s, dz - 1], zr.at[s, dz - 1], z_s.at[s, dz - 1], z_r.at[s, dz - 1],
            fdev(x, (zl + dz) % 4, c),
        )

    def tp_copies(view, ss, rs):
        own = view(t)
        other = view((1 - zh) * 4 + y)
        first = [remote(own, own, ss(0), rs(0), tdev(1 - zh, y))]
        first += [remote(own, own, ss(d), rs(d), tdev(zh, (y + d) % 4)) for d in FAR]
        second = [remote(other, other, ss(3 + d), rs(3 + d), tdev(zh, (y + d) % 4)) for d in FAR]
        return first, second

    left_first, left_second = tp_copies(
        lambda k: left.at[:, :, pl.ds(pl.multiple_of(k * 64, 64), 64), :],
        lambda i: l_s.at[i], lambda i: l_r.at[i],
    )
    g_copies = [
        tp_copies(lambda k, s=s: ag.at[s, k], lambda i, s=s: g_s.at[s, i], lambda i, s=s: g_r.at[s, i])
        for s in range(2)
    ]
    h_copies = [
        tp_copies(lambda k, s=s: ah.at[s, k], lambda i, s=s: h_s.at[s, i], lambda i, s=s: h_r.at[s, i])
        for s in range(2)
    ]

    def right_copy(d):
        k = (t + d) % 8
        rows = rc.at[:, pl.ds(pl.multiple_of(t * 64, 64), 64), :]
        return remote(rmsg.at[k], rows, r_s.at[d], r_r.at[d], (f, k))

    def a2a_copy(d):
        k = (f + d) % 32
        return remote(a2s.at[k], a2r.at[f], a_s.at[d], a_r.at[d], (k, t))

    def start(copies):
        for cp in copies:
            cp.start()

    loads[0].wait()
    own_rows = pl.ds(pl.multiple_of(t * 64, 64), 64)
    for s in range(2):
        high, low = split(bl[s])
        left[s, 0, own_rows, :] = high
        left[s, 1, own_rows, :] = low
    loads[1].wait()
    lanes = lane_iota(64)
    for u in range(4):
        a = br[0, :, u * 128 : u * 128 + 128]
        b = br[1, :, u * 128 : u * 128 + 128]
        for k, v in ((2 * u, jnp.where(lanes < 64, a, roll_half(b))), (2 * u + 1, jnp.where(lanes < 64, roll_half(a), b))):
            high, low = split(v)
            rmsg[k, 0] = high
            rmsg[k, 1] = low
    rc[:, own_rows, :] = rmsg[t]

    pl.semaphore_wait(barrier, 38)
    start(left_first)

    @pl.loop(1, 8)
    def _(d):
        right_copy(d).start()

    def extract(slot):
        b = bos[slot]
        half = b % 2
        pair = b // 2
        near = g[pair * 2 + half]
        away = g[pair * 2 + 1 - half]
        upper = (lane_iota(256) >= 64).astype(i32)
        return jnp.where(upper == half, near, roll_half(away))

    def slot_of(s, dx, z, core):
        return ((((x + dx) % 4) * 4 + z) * 2 + core) * 2 + s

    def core_stage(s):
        for dx in (2, 1, 3, 0):

            @pl.loop(0, 4)
            def _(z):
                cs[s, dx, z] = extract(slot_of(s, dx, z, 1 - c))

            core_copy(s, dx).start()

    def x_stage(s):
        for dx in FAR:
            core_copy(s, dx).wait_recv()

            @pl.loop(0, 4)
            def _(i):
                z = (zl + 1 + i) % 4
                encode(extract(slot_of(s, dx, z, c)) + cr[s, dx, z], xs.at[s, dx - 1, z])
                x_copy(s, dx, z).start()

    def x_sum(s, z):
        for dx in FAR:
            x_copy(s, dx, z).wait_recv()
        total = extract(slot_of(s, 0, z, c)) + cr[s, 0, z]
        for dx in FAR:
            total += decode(xr.at[s, dx - 1, z])
        return total

    def z_stage(s):
        core_copy(s, 0).wait_recv()

        @pl.loop(1, 4)
        def _(dz):
            encode(x_sum(s, (zl + dz) % 4), zs.at[s, dz - 1])
            z_copy(s, dz).start()

        za[s] = x_sum(s, zl)

    def g_stage(s):
        total = za[s]
        for dz in range(1, 4):
            z_copy(s, dz).wait_recv()
            total += decode(zr.at[s, dz - 1])
        turned = total.T
        a, b = turned[0:64], turned[64:128]
        gslab[s, :, 0:256] = a
        gslab[s, :, 256:512] = b
        encode(jnp.concatenate([a[:, :128], a[:, 128:], b[:, :128], b[:, 128:]], axis=0), ag.at[s, t])
        start(g_copies[s][0])

    def forward(copies):
        copies[0][0].wait_recv()
        start(copies[1])

    def gathered(copies, messages, s, store):
        for cp in copies[0][1:] + copies[1]:
            cp.wait_recv()

        @pl.loop(0, 8)
        def _(k):
            v = decode(messages.at[s, k])
            rows = pl.ds(pl.multiple_of(k * 64, 64), 64)
            for q in range(4):
                high, low = split(v[q * 64 : q * 64 + 64])
                store[s, 0, rows, q * 128 : q * 128 + 128] = high
                store[s, 1, rows, q * 128 : q * 128 + 128] = low

    def put(ref, dst, i, s):
        return pltpu.make_async_copy(ref.at[s], dst.at[s], out_sem.at[i, s])

    def rotate(s):
        gathered(g_copies[s], ag, s, gt)
        partial = dot3(br[s], gt[s, 0], gt[s, 1], PLAIN)
        rotated = dot3(partial, left[s, 0], left[s, 1], MINOR)
        new_moment = first_decay * mo[s] + (1.0 - first_decay) * rotated
        new_second = second_decay * se[s] + (1.0 - second_decay) * rotated * rotated
        mo[s] = new_moment
        se[s] = new_second
        direction = new_moment / (jnp.sqrt(new_second) + epsilon)
        half = dot3(direction, left[s, 0], left[s, 1], PLAIN)
        encode(jnp.concatenate([half[:, q * 128 : q * 128 + 128] for q in range(4)], axis=0), ah.at[s, t])
        start(h_copies[s][0])
        put(mo, nm_h, 0, s).start()
        put(se, ns_h, 1, s).start()

    def statistics(s):
        right = dot3(gslab[s], gt[s, 0], gt[s, 1], MINOR)
        sr[s] = second_decay * sr[s] + (1.0 - second_decay) * right
        put(sr, nr_h, 2, s).start()
        cols = pl.ds(pl.multiple_of((t // 2) * 128, 128), 128)
        rows = gt[s, 0, :, cols].astype(f32) + gt[s, 1, :, cols].astype(f32)
        tmp[...] = rows.T
        mine = tmp[pl.ds(pl.multiple_of((t % 2) * 64, 64), 64), :]
        out = dot3(mine, gt[s, 0], gt[s, 1], PLAIN)
        sl[s] = second_decay * sl[s] + (1.0 - second_decay) * out
        put(sl, nl_h, 3, s).start()

    def back(s):
        gathered(h_copies[s], ah, s, hb)
        bk[pl.ds(s * 64, 64), :] = dot3(rct[pl.ds(s * 64, 64), :], hb[s, 0], hb[s, 1], PLAIN)

    @pl.loop(0, 32)
    def _(i):
        grad_load(i).wait()

    core_stage(0)
    x_stage(0)
    core_stage(1)
    x_stage(1)
    forward((left_first, left_second))
    z_stage(0)
    for cp in loads[2:]:
        cp.wait()

    @pl.loop(1, 8)
    def _(d):
        right_copy(d).wait_recv()

    rct[...] = (rc[0].astype(f32) + rc[1].astype(f32)).T
    g_stage(0)
    z_stage(1)
    forward(g_copies[0])
    g_stage(1)
    for cp in left_first[1:] + left_second:
        cp.wait_recv()
    rotate(0)
    forward(g_copies[1])
    rotate(1)
    forward(h_copies[0])
    statistics(0)
    forward(h_copies[1])
    statistics(1)
    back(0)
    back(1)
    rows = bk[...].T.astype(bf16)
    for k in range(32):
        a2s[k] = rows[k * 16 : k * 16 + 16]
    a2r[f] = a2s[f]

    @pl.loop(1, 32)
    def _(d):
        a2a_copy(d).start()

    for s in range(2):
        for dx in range(4):
            core_copy(s, dx).wait_send()
        for dx in FAR:

            @pl.loop(0, 4)
            def _(z):
                x_copy(s, dx, z).wait_send()

        for dz in range(1, 4):
            z_copy(s, dz).wait_send()
        for cp in g_copies[s][0] + g_copies[s][1] + h_copies[s][0] + h_copies[s][1]:
            cp.wait_send()
        for i, (ref, dst) in enumerate(((mo, nm_h), (se, ns_h), (sr, nr_h), (sl, nl_h))):
            put(ref, dst, i, s).wait()
    for cp in left_first + left_second:
        cp.wait_send()

    @pl.loop(1, 8)
    def _(d):
        right_copy(d).wait_send()

    @pl.loop(1, 32)
    def _(d):
        a2a_copy(d).wait()

    low_lanes = lane_iota(16) < 64

    @pl.loop(0, 4)
    def _(p):
        for u in range(8):
            first, second = inv[p * 16 + 2 * u], inv[p * 16 + 2 * u + 1]
            a = a2r[first // 2].astype(f32)
            b = a2r[second // 2].astype(f32)
            a = jnp.where((lane_iota(16) * 0 + first % 2) == 0, a, roll_half(a))
            b = jnp.where((lane_iota(16) * 0 + second % 2) == 1, b, roll_half(b))
            upd[p, :, u * 128 : u * 128 + 128] = jnp.where(low_lanes, a, b).astype(bf16)

    cp = pltpu.make_async_copy(upd, upd_h, loc.at[6])
    cp.start()
    cp.wait()


def local(grad_part, block_of_slot, stat_left, stat_right, basis_left, basis_right, moment, second):
    order = jnp.arange(64, dtype=i32)
    inverse = jnp.sum(jnp.where(block_of_slot[None, :] == order[:, None], order[None, :], 0), axis=1)
    smem = pl.BlockSpec(memory_space=pltpu.SMEM)
    hbm = pl.BlockSpec(memory_space=pl.ANY)
    state = jax.ShapeDtypeStruct((2, 64, 512), f32)
    v = pltpu.VMEM
    dma = pltpu.SemaphoreType.DMA
    return pl.pallas_call(
        kernel,
        name="step",
        out_shape=(jax.ShapeDtypeStruct((4, 16, 1024), bf16), state, state, state, state),
        in_specs=[smem, smem] + [hbm] * 7,
        out_specs=(hbm,) * 5,
        scratch_shapes=[
            v((64, 256, 128), f32),
            *[v((2, 64, 512), f32)] * 6,
            v((4, 16, 1024), bf16),
            v((2, 4, 4, 256, 128), f32),
            v((2, 4, 4, 256, 128), f32),
            v((2, 3, 4, 272, 128), i16),
            v((2, 3, 4, 272, 128), i16),
            v((2, 3, 272, 128), i16),
            v((2, 3, 272, 128), i16),
            v((2, 256, 128), f32),
            v((2, 64, 512), f32),
            v((2, 8, 272, 128), i16),
            v((2, 8, 272, 128), i16),
            v((2, 2, 512, 512), bf16),
            v((8, 2, 64, 128), bf16),
            v((2, 512, 128), bf16),
            v((128, 512), f32),
            v((2, 2, 512, 512), bf16),
            v((2, 2, 512, 512), bf16),
            v((128, 512), f32),
            v((128, 512), f32),
            v((32, 16, 128), bf16),
            v((32, 16, 128), bf16),
            dma((8,)),
            dma((32,)),
            dma((4, 2)),
            *[dma((2, 4))] * 2,
            *[dma((2, 3, 4))] * 2,
            *[dma((2, 3))] * 2,
            *[dma((7,))] * 2,
            *[dma((8,))] * 2,
            *[dma((2, 7))] * 4,
            *[dma((32,))] * 2,
        ],
        compiler_params=pltpu.CompilerParams(
            collective_id=0, has_side_effects=True, vmem_limit_bytes=52 * 2**20
        ),
    )(block_of_slot, inverse, grad_part.reshape(4, 2, 256, 1024), stat_left, stat_right, basis_left, basis_right, moment, second)


def solution(mesh):
    return jax.shard_map(
        local,
        mesh=mesh,
        in_specs=(
            P("fsdp", None, None, "tp"),
            P(),
            P("fsdp", "tp", None),
            P("fsdp", "tp", None),
            P("fsdp", "tp", None),
            P("fsdp", "tp", None),
            P("fsdp", "tp", None),
            P("fsdp", "tp", None),
        ),
        out_specs=(
            P(None, "fsdp", "tp"),
            P("fsdp", "tp", None),
            P("fsdp", "tp", None),
            P("fsdp", "tp", None),
            P("fsdp", "tp", None),
        ),
        check_vma=False,
    )
```

time: 502 us -> 94.1 us (0.19)
  waiting for transfers between devices: 310 us -> 0 us
  blocking collectives: 128 us -> 0 us
  Pallas kernels: 0 us -> 85.5 us
  starting transfers between devices: 19.4 us -> 0 us
  matrix products: 15.3 us -> 0 us
  between operations: 14.7 us -> 0.66 us
  local copies, waits for them, and re-layouts: 12.4 us -> 6.97 us
    reduce_scatter x1 -> x0, waiting for transfers between devices: 165 us -> none  [local(): lax.psum_scatter(grad_part[0], 'fsdp', scatter_dimension=1, tiled=True)]
    all_gather x2 -> x0, waiting for transfers between devices: 141 us -> none  [the longest x1 71.4 us: local(): left_rows = lax.all_gather(basis_left, 'tp', axis=1, tiled=True)]
    unnamed x1 -> x0, blocking collectives: 109 us -> none
    pallas_call x0 -> x1, Pallas kernels: none -> 85.5 us  [local(): pl.pallas_call(kernel, name='step', out_shape=(jax.ShapeDtypeStruct((4, 1...]
    all_to_all x1 -> x0, starting transfers between devices: 19.3 us -> none  [local(): lax.all_to_all(update_cols, 'fsdp', split_axis=2, concat_axis=0, tiled=True)]
    all_to_all x1 -> x0, blocking collectives: 19.1 us -> none  [local(): lax.all_to_all(by_slot, 'fsdp', split_axis=0, concat_axis=2, tiled=True)]
    dot_general x6 -> x0, matrix products: 15.3 us -> none  [product(): jnp.einsum(form, left, right, precision=highest, preferred_element_type=j...]
  transfers between devices with their start and end apart: 4 -> 0, of which waited for: 4 -> 0; matrix products, arithmetic and copies ran while one was open for 2% -> 0% of each run, Pallas kernels for 0% -> 0%
where the time goes in v1:
time: 94.1 us; the launch traced here: 93.9 us
  Pallas kernels  85.5 us (91%)
  local copies, waits for them, and re-layouts  6.97 us (7%)
    pallas_call x1, Pallas kernels, local(): pl.pallas_call(kernel, name='step', out_shape=(jax.ShapeDtypeStruct((4, 1...  85.5 us
    unnamed x13, local copies, waits for them, and re-layouts  6.97 us

profile of v1, /device:TPU:1, one launch (start us, length us, event | category | flops | bytes accessed | tf_op | source)
XLA Modules:
  0.0 93.9 jit_solution(12484219830960883004)
XLA Ops:
  0.6 0.8 select_reduce_fusion.inv
  1.4 0.0 copy-start
  1.4 0.9 %copy-done = f32[2,64,512]{2,1,0:T(8,128)S(1)} copy-done((f32[2,64,512]{2,1,0:T(8,128)S(1)}, f32[2,64,512]{2,1,0:T(8,128)}, u32[]{:S(2)}) %copy-start) | copy-done | bytes 262168
  2.4 0.0 copy-start.1
  2.4 0.9 %copy-done.1 = f32[2,64,512]{2,1,0:T(8,128)S(1)} copy-done((f32[2,64,512]{2,1,0:T(8,128)S(1)}, f32[2,64,512]{2,1,0:T(8,128)}, u32[]{:S(2)}) %copy-start.1) | copy-done | bytes 262168
  3.3 0.0 copy-start.2
  3.3 0.9 %copy-done.2 = f32[2,64,512]{2,1,0:T(8,128)S(1)} copy-done((f32[2,64,512]{2,1,0:T(8,128)S(1)}, f32[2,64,512]{2,1,0:T(8,128)}, u32[]{:S(2)}) %copy-start.2) | copy-done | bytes 262168
  4.3 0.0 copy-start.3
  4.3 0.7 copy-done.3
  4.9 85.5 %step.1 = (bf16[4,16,1024]{2,1,0:T(8,128)(2,1)S(1)}, f32[2,64,512]{2,1,0:T(8,128)S(1)}, f32[2,64,512]{2,1,0:T(8,128)S(1)}, f32[2,64,512]{2,1,0:T(8,128)S(1)}, f32[2,64,512]{2,1,0:T(8,128)S(1)}) custom-call(s32[64]{0:T(128)S(1)} %copy-done.3, s32[64]{0:T(128)S(1)} %select_reduce_fusion.inv, f32[4,2,256,1024]{3,2,1,0:T(8,128)} %bitcast.1, ...), custom_call_target="tpu_custom_call" | custom-call | tf_op jit(solution)/shard_map/step/pallas_call | solution.py:389
  90.4 0.7 copy.18
  91.1 0.7 copy.19
  91.8 0.7 copy.20
  92.5 0.7 copy.21
  93.2 0.7 copy.22
Async XLA Ops:
  1.4 1.0 %copy-start = (f32[2,64,512]{2,1,0:T(8,128)S(1)}, f32[2,64,512]{2,1,0:T(8,128)}, u32[]{:S(2)}) copy-start(f32[2,64,512]{2,1,0:T(8,128)} %sl_h.1) | copy-start | bytes 786436
  2.4 0.9 %copy-start.1 = (f32[2,64,512]{2,1,0:T(8,128)S(1)}, f32[2,64,512]{2,1,0:T(8,128)}, u32[]{:S(2)}) copy-start(f32[2,64,512]{2,1,0:T(8,128)} %sr_h.1) | copy-start | bytes 786436
  3.3 0.9 %copy-start.2 = (f32[2,64,512]{2,1,0:T(8,128)S(1)}, f32[2,64,512]{2,1,0:T(8,128)}, u32[]{:S(2)}) copy-start(f32[2,64,512]{2,1,0:T(8,128)} %bl_h.1) | copy-start | bytes 786436
  4.3 0.7 copy-start.3

commit v2 on v1

v2 whole, which is shorter than its diff:
```python
import jax
import jax.numpy as jnp
from jax import lax
from jax.experimental import pallas as pl
from jax.experimental.pallas import tpu as pltpu
from jax.sharding import PartitionSpec as P

first_decay = 0.9
second_decay = 0.95
epsilon = 1e-08
MESH = pl.DeviceIdType.MESH
f32, bf16, i16, i32 = jnp.float32, jnp.bfloat16, jnp.int16, jnp.int32
FAR = (2, 1, 3)
vmem_bytes = 64 * 2**20 - 19 * 2**16


def roll_half(v):
    return pltpu.roll(v, 64, 1)


def lane_iota(rows):
    return lax.broadcasted_iota(i32, (rows, 128), 1)


def split(v):
    high = v.astype(bf16)
    return high, (v - high.astype(f32)).astype(bf16)


def dot(a, b, dims):
    return lax.dot_general(a, b, (dims, ((), ())), preferred_element_type=f32)


PLAIN = ((1,), (0,))
MINOR = ((1,), (1,))


def dot3(a, bh, bl, dims):
    ah, al = split(a)
    return dot(ah, bh, dims) + (dot(ah, bl, dims) + dot(al, bh, dims))


def encode(v, ref):
    top = jnp.max(jnp.abs(v), axis=0, keepdims=True)
    power = jnp.ceil(jnp.log2(jnp.maximum(top, 1e-30) * (1.0 / 32500.0)))
    ref[pl.ds(0, 256), :] = jnp.round(v * jnp.exp2(-power)).astype(i32).astype(i16)
    ref[pl.ds(256, 16), :] = jnp.broadcast_to(power, (16, 128)).astype(i32).astype(i16)


def scale_of(ref):
    return jnp.exp2(ref[pl.ds(256, 16), :].astype(i32).astype(f32))[0:1]


def decode(ref):
    return ref[pl.ds(0, 256), :].astype(i32).astype(f32) * scale_of(ref)


def kernel(
    bos, grad_h, sl_h, sr_h, bl_h, br_h, mo_h, se_h,
    a2r, nl, nr, nm, ns,
    g, sl, sr, bl, br, mo, se,
    cs, cr, xq, xqr, xs, xr, zs, zr, za, gslab, ag, ah, lm, left, rmsg, rc, rct, gt, hb, tmp, bk, part, a2s,
    loc, g_sem, out_sem, c_s, c_r, q_s, q_r, x_s, x_r, z_s, z_r, l_s, l_r, r_s, r_r, g_s, g_r, h_s, h_r, a_s, a_r,
):
    f = lax.axis_index("fsdp")
    t = lax.axis_index("tp")
    x, zl, c = f // 8, (f // 2) % 4, f % 2
    zh, y = t // 4, t % 4

    def fdev(x_, z_, c_):
        return ((x_ * 4 + z_) * 2 + c_, t)

    def tdev(zh_, y_):
        return (f, zh_ * 4 + y_)

    def remote(src, dst, ss, rs, dev):
        return pltpu.make_async_remote_copy(
            src_ref=src, dst_ref=dst, send_sem=ss, recv_sem=rs, device_id=dev, device_id_type=MESH
        )

    loads = [
        pltpu.make_async_copy(src, dst, loc.at[i])
        for i, (src, dst) in enumerate(((bl_h, bl), (br_h, br), (sl_h, sl), (sr_h, sr), (mo_h, mo), (se_h, se)))
    ]

    def grad_load(i):
        return pltpu.make_async_copy(
            grad_h.at[:, :, pl.ds(pl.multiple_of(i * 128, 128), 128)], g.at[pl.ds(8 * i, 8)], g_sem.at[i]
        )

    @pl.loop(0, 8)
    def _(i):
        grad_load(i).start()

    for cp in loads:
        cp.start()

    barrier = pltpu.get_barrier_semaphore()

    @pl.loop(1, 32)
    def _(d):
        pl.semaphore_signal(barrier, inc=1, device_id=((f + d) % 32, t), device_id_type=MESH)

    @pl.loop(1, 8)
    def _(d):
        pl.semaphore_signal(barrier, inc=1, device_id=(f, (t + d) % 8), device_id_type=MESH)

    def core_copy(s, dx):
        return remote(cs.at[s, dx], cr.at[s, dx], c_s.at[s, dx], c_r.at[s, dx], fdev(x, zl, 1 - c))

    def relay_copy(s, i):
        return remote(
            xq.at[s, i], xqr.at[s, i], q_s.at[s, i], q_r.at[s, i], fdev((x + 1 + i // 2 * 2) % 4, zl, c)
        )

    def x_copy(s, way, i):
        return remote(
            xs.at[s, way, i], xr.at[s, way, i], x_s.at[s, way, i], x_r.at[s, way, i],
            fdev((x + 1 + 2 * way) % 4, zl, c),
        )

    def z_copy(s, dz):
        return remote(
            zs.at[s, dz - 1], zr.at[s, dz - 1], z_s.at[s, dz - 1], z_r.at[s, dz - 1],
            fdev(x, (zl + dz) % 4, c),
        )

    def tp_copies(view, ss, rs):
        own = view(t)
        other = view((1 - zh) * 4 + y)
        first = [remote(own, own, ss(0), rs(0), tdev(1 - zh, y))]
        first += [remote(own, own, ss(d), rs(d), tdev(zh, (y + d) % 4)) for d in FAR]
        second = [remote(other, other, ss(3 + d), rs(3 + d), tdev(zh, (y + d) % 4)) for d in FAR]
        return first, second

    left_first, left_second = tp_copies(lambda k: lm.at[k], lambda i: l_s.at[i], lambda i: l_r.at[i])
    g_copies = [
        tp_copies(lambda k, s=s: ag.at[s, k], lambda i, s=s: g_s.at[s, i], lambda i, s=s: g_r.at[s, i])
        for s in range(2)
    ]
    h_copies = [
        tp_copies(lambda k, s=s: ah.at[s, k], lambda i, s=s: h_s.at[s, i], lambda i, s=s: h_r.at[s, i])
        for s in range(2)
    ]

    def right_copy(d):
        k = (t + d) % 8
        return remote(rmsg.at[k], rc.at[t], r_s.at[d], r_r.at[d], (f, k))

    def a2a_copy(d):
        k = (f + d) % 32
        return remote(a2s.at[k], a2r.at[f], a_s.at[d], a_r.at[d], (k, t))

    def start(copies):
        for cp in copies:
            cp.start()

    leaving = {}

    def left_device(*name):
        leaving.pop(name)()

    def wait_sent(copies):
        for cp in copies:
            cp.wait_send()

    pl.semaphore_wait(barrier, 38)

    def stacked(v):
        return jnp.concatenate([v[:, q * 128 : q * 128 + 128] for q in range(4)], axis=0)

    def send_left():
        loads[0].wait()
        for s in range(2):
            encode(stacked(bl[s]), lm.at[t, s])
        start(left_first)
        leaving["left", 0] = lambda: wait_sent(left_first)

    def send_right():
        lanes = lane_iota(64)
        for u in range(4):
            a = br[0, :, u * 128 : u * 128 + 128]
            b = br[1, :, u * 128 : u * 128 + 128]
            even, odd = jnp.where(lanes < 64, a, roll_half(b)), jnp.where(lanes < 64, roll_half(a), b)
            for k, v in ((2 * u, even), (2 * u + 1, odd)):
                high, low = split(v)
                rmsg[k, 0] = high
                rmsg[k, 1] = low
        rc[t] = rmsg[t]

        @pl.loop(1, 8)
        def _(d):
            right_copy(d).start()

        def sent():
            @pl.loop(1, 8)
            def _(d):
                right_copy(d).wait_send()

        leaving["right",] = sent

    def extract(slot):
        b = bos[slot]
        half = b % 2
        first = ((b % 16) // 2 * 4 + b // 16) * 2
        near = g[first + half]
        away = g[first + 1 - half]
        upper = (lane_iota(256) >= 64).astype(i32)
        return jnp.where(upper == half, near, roll_half(away))

    def slot_of(s, dx, z, core):
        return ((((x + dx) % 4) * 4 + z) * 2 + core) * 2 + s

    def core_part(s, dx):
        @pl.loop(0, 4)
        def _(z):
            cs[s, dx, z] = extract(slot_of(s, dx, z, 1 - c))

        core_copy(s, dx).start()
        leaving["core", s, dx] = lambda: core_copy(s, dx).wait_send()

    def pair_sum(s, dx, z):
        return extract(slot_of(s, dx, z, c)) + cr[s, dx, z]

    def relay_stage(s):
        core_copy(s, 2).wait_recv()

        @pl.loop(0, 4)
        def _(j):
            i = j // 2 + 2 * (j % 2)
            encode(pair_sum(s, 2, (zl + 1 + i) % 4), xq.at[s, i])
            relay_copy(s, i).start()

        def sent():
            @pl.loop(0, 4)
            def _(i):
                relay_copy(s, i).wait_send()

        leaving["relay", s] = sent

    def near_stage(s, j):
        for way in (1, 0):
            if j == 0:
                core_copy(s, 1 + 2 * way).wait_recv()
            i = j + 2 - 2 * way
            encode(pair_sum(s, 1 + 2 * way, (zl + 1 + i) % 4), xs.at[s, way, i])
            x_copy(s, way, i).start()
        leaving["near", s, j] = lambda: wait_sent([x_copy(s, 1, j), x_copy(s, 0, j + 2)])

    def relayed_stage(s, j):
        for way in (0, 1):
            i = j + 2 * way
            own = pair_sum(s, 1 + 2 * way, (zl + 1 + i) % 4)
            relay_copy(s, i).wait_recv()
            encode(own + decode(xqr.at[s, i]), xs.at[s, way, i])
            x_copy(s, way, i).start()
        leaving["relayed", s, j] = lambda: wait_sent([x_copy(s, 0, j), x_copy(s, 1, j + 2)])

    def x_sum(s, i):
        total = pair_sum(s, 0, (zl + 1 + i) % 4)
        for way in range(2):
            x_copy(s, way, i).wait_recv()
            total += decode(xr.at[s, way, i])
        return total

    def z_send(s, dz):
        if dz == 1:
            core_copy(s, 0).wait_recv()
        encode(x_sum(s, dz - 1), zs.at[s, dz - 1])
        z_copy(s, dz).start()
        leaving["z", s, dz] = lambda: z_copy(s, dz).wait_send()

    def z_keep(s):
        za[s] = x_sum(s, 3)

    def g_stage(s):
        total = za[s]
        for dz in range(1, 4):
            z_copy(s, dz).wait_recv()
            total += decode(zr.at[s, dz - 1])
        turned = total.T
        a, b = turned[0:64], turned[64:128]
        gslab[s, :, 0:256] = a
        gslab[s, :, 256:512] = b
        encode(jnp.concatenate([a[:, :128], a[:, 128:], b[:, :128], b[:, 128:]], axis=0), ag.at[s, t])
        start(g_copies[s][0])
        leaving["g", s] = lambda: wait_sent(g_copies[s][0])

    def forward(name, s, copies):
        copies[0][0].wait_recv()
        start(copies[1])
        leaving["forward", name, s] = lambda: wait_sent(copies[1])

    def unpack(message, s, store, half):
        @pl.loop(0, 4)
        def _(j):
            k = half * 4 + j
            v = decode(message(k))
            rows = pl.ds(pl.multiple_of(k * 64, 64), 64)
            for q in range(4):
                high, low = split(v[q * 64 : q * 64 + 64])
                store[s, 0, rows, q * 128 : q * 128 + 128] = high
                store[s, 1, rows, q * 128 : q * 128 + 128] = low

    def half_product(a, store, s, half):
        k = pl.ds(pl.multiple_of(half * 256, 256), 256)
        return dot3(a[:, k], store[s, 0, k, :], store[s, 1, k, :], PLAIN)

    def near_half(copies, messages, s, store, a):
        for cp in copies[0][1:]:
            cp.wait_recv()
        unpack(lambda k: messages.at[s, k], s, store, zh)
        part[s] = half_product(a, store, s, zh)

    def far_half(copies, messages, s, store, a):
        for cp in copies[1]:
            cp.wait_recv()
        unpack(lambda k: messages.at[s, k], s, store, 1 - zh)
        return part[s] + half_product(a, store, s, 1 - zh)

    def put(ref, dst, i, s):
        return pltpu.make_async_copy(ref.at[s], dst.at[s], out_sem.at[i, s])

    def rotate_near(s):
        near_half(g_copies[s], ag, s, gt, br.at[s])

    def rotate(s):
        partial = far_half(g_copies[s], ag, s, gt, br.at[s])
        rotated = dot3(partial, left[s, 0], left[s, 1], MINOR)
        new_moment = first_decay * mo[s] + (1.0 - first_decay) * rotated
        new_second = second_decay * se[s] + (1.0 - second_decay) * rotated * rotated
        mo[s] = new_moment
        se[s] = new_second
        direction = new_moment / (jnp.sqrt(new_second) + epsilon)
        half = dot3(direction, left[s, 0], left[s, 1], PLAIN)
        encode(stacked(half), ah.at[s, t])
        start(h_copies[s][0])
        leaving["h", s] = lambda: wait_sent(h_copies[s][0])
        put(mo, nm, 0, s).start()
        put(se, ns, 1, s).start()

    def statistics(s):
        right = dot3(gslab[s], gt[s, 0], gt[s, 1], MINOR)
        sr[s] = second_decay * sr[s] + (1.0 - second_decay) * right
        put(sr, nr, 2, s).start()
        cols = pl.ds(pl.multiple_of((t // 2) * 128, 128), 128)
        rows = gt[s, 0, :, cols].astype(f32) + gt[s, 1, :, cols].astype(f32)
        tmp[...] = rows.T
        mine = tmp[pl.ds(pl.multiple_of((t % 2) * 64, 64), 64), :]
        out = dot3(mine, gt[s, 0], gt[s, 1], PLAIN)
        sl[s] = second_decay * sl[s] + (1.0 - second_decay) * out
        put(sl, nl, 3, s).start()

    def back_near(s):
        near_half(h_copies[s], ah, s, hb, rct.at[pl.ds(s * 64, 64)])

    def back(s):
        bk[pl.ds(s * 64, 64), :] = far_half(h_copies[s], ah, s, hb, rct.at[pl.ds(s * 64, 64)])

    def grad_ready():
        @pl.loop(0, 8)
        def _(i):
            grad_load(i).wait()

    def right_ready():
        @pl.loop(1, 8)
        def _(d):
            right_copy(d).wait_recv()

        rct[...] = jnp.concatenate([rc[k, 0].astype(f32) + rc[k, 1].astype(f32) for k in range(8)], axis=0).T

    def left_ready():
        for cp in loads[1:]:
            cp.wait()
        for cp in left_first[1:] + left_second:
            cp.wait_recv()
        for s in range(2):
            unpack(lambda k: lm.at[k, s], s, left, 0)
            unpack(lambda k: lm.at[k, s], s, left, 1)

    def send_back():
        rows = bk[...].T.astype(bf16)
        for k in range(32):
            a2s[k] = rows[k * 16 : k * 16 + 16]

        @pl.loop(0, 31)
        def _(d):
            a2a_copy((d + 15) % 31 + 1).start()

        a2r[f] = a2s[f]

    steps = [
        lambda: grad_ready(),
        lambda: core_part(0, 2),
        lambda: core_part(0, 3),
        lambda: core_part(0, 1),
        lambda: send_left(),
        lambda: relay_stage(0),
        lambda: core_part(0, 0),
        lambda: core_part(1, 2),
        lambda: near_stage(0, 0),
        lambda: near_stage(0, 1),
        lambda: core_part(1, 3),
        lambda: relayed_stage(0, 0),
        lambda: relayed_stage(0, 1),
        lambda: core_part(1, 1),
        lambda: left_device("near", 0, 0),
        lambda: left_device("near", 0, 1),
        lambda: relay_stage(1),
        lambda: core_part(1, 0),
        lambda: z_send(0, 1),
        lambda: z_send(0, 3),
        lambda: z_send(0, 2),
        lambda: z_keep(0),
        lambda: near_stage(1, 0),
        lambda: near_stage(1, 1),
        lambda: relayed_stage(1, 0),
        lambda: relayed_stage(1, 1),
        lambda: forward("left", 0, (left_first, left_second)),
        lambda: g_stage(0),
        lambda: z_send(1, 1),
        lambda: z_send(1, 3),
        lambda: z_send(1, 2),
        lambda: z_keep(1),
        lambda: left_ready(),
        lambda: forward("g", 0, g_copies[0]),
        lambda: rotate_near(0),
        lambda: g_stage(1),
        lambda: rotate(0),
        lambda: forward("g", 1, g_copies[1]),
        lambda: send_right(),
        lambda: rotate_near(1),
        lambda: rotate(1),
        lambda: forward("h", 0, h_copies[0]),
        lambda: statistics(0),
        lambda: right_ready(),
        lambda: forward("h", 1, h_copies[1]),
        lambda: back_near(0),
        lambda: back(0),
        lambda: statistics(1),
        lambda: back_near(1),
        lambda: back(1),
        lambda: send_back(),
    ]
    for step in steps:
        step()

    for sent in list(leaving.values()):
        sent()
    for s in range(2):
        for i, (ref, dst) in enumerate(((mo, nm), (se, ns), (sr, nr), (sl, nl))):
            put(ref, dst, i, s).wait()

    @pl.loop(1, 32)
    def _(d):
        a2a_copy(d).wait()


def finish(bos, rows, nl, nr, nm, ns, upd_out, nl_out, nr_out, nm_out, ns_out, upd, sem):
    outs = [
        pltpu.make_async_copy(src, dst, sem.at[i])
        for i, (src, dst) in enumerate(((nl, nl_out), (nr, nr_out), (nm, nm_out), (ns, ns_out), (upd, upd_out)))
    ]
    for out in outs[:4]:
        out.start()

    upper = lane_iota(16) >= 64

    @pl.loop(0, 16)
    def _(k):
        for u in range(2):
            both = rows[2 * k + u].astype(f32)
            turned = roll_half(both)
            for j in range(2):
                b = bos[4 * k + 2 * u + j]
                half = b % 2
                cols = pl.ds(pl.multiple_of(b % 16 // 2 * 128, 128), 128)
                old = upd[b // 16, :, cols]
                new = jnp.where((lane_iota(16) * 0 + half) == j, both, turned).astype(bf16)
                upd[b // 16, :, cols] = jnp.where(upper == ((lane_iota(16) * 0 + half) == 1), new, old)

    outs[4].start()
    for out in outs:
        out.wait()


def local(grad_part, block_of_slot, stat_left, stat_right, basis_left, basis_right, moment, second):
    smem = pl.BlockSpec(memory_space=pltpu.SMEM)
    hbm = pl.BlockSpec(memory_space=pl.ANY)
    state = jax.ShapeDtypeStruct((2, 64, 512), f32)
    vmem = pl.BlockSpec(memory_space=pltpu.VMEM)
    v = pltpu.VMEM
    dma = pltpu.SemaphoreType.DMA
    outs = pl.pallas_call(
        kernel,
        name="step",
        out_shape=(jax.ShapeDtypeStruct((32, 16, 128), bf16), state, state, state, state),
        in_specs=[smem] + [hbm] * 7,
        out_specs=(vmem, hbm, hbm, hbm, hbm),
        scratch_shapes=[
            v((64, 256, 128), f32),
            *[v((2, 64, 512), f32)] * 6,
            v((2, 4, 4, 256, 128), f32),
            v((2, 4, 4, 256, 128), f32),
            v((2, 4, 272, 128), i16),
            v((2, 4, 272, 128), i16),
            v((2, 2, 4, 272, 128), i16),
            v((2, 2, 4, 272, 128), i16),
            v((2, 3, 272, 128), i16),
            v((2, 3, 272, 128), i16),
            v((2, 256, 128), f32),
            v((2, 64, 512), f32),
            v((2, 8, 272, 128), i16),
            v((2, 8, 272, 128), i16),
            v((8, 2, 272, 128), i16),
            v((2, 2, 512, 512), bf16),
            v((8, 2, 64, 128), bf16),
            v((8, 2, 64, 128), bf16),
            v((128, 512), f32),
            v((2, 2, 512, 512), bf16),
            v((2, 2, 512, 512), bf16),
            v((128, 512), f32),
            v((128, 512), f32),
            v((2, 64, 512), f32),
            v((32, 16, 128), bf16),
            dma((6,)),
            dma((8,)),
            dma((4, 2)),
            *[dma((2, 4))] * 4,
            *[dma((2, 2, 4))] * 2,
            *[dma((2, 3))] * 2,
            *[dma((7,))] * 2,
            *[dma((8,))] * 2,
            *[dma((2, 7))] * 4,
            *[dma((32,))] * 2,
        ],
        compiler_params=pltpu.CompilerParams(
            collective_id=0, has_side_effects=True, vmem_limit_bytes=vmem_bytes
        ),
    )(block_of_slot, grad_part.reshape(8, 256, 1024), stat_left, stat_right, basis_left, basis_right, moment, second)
    return pl.pallas_call(
        finish,
        name="finish",
        out_shape=(jax.ShapeDtypeStruct((4, 16, 1024), bf16), state, state, state, state),
        in_specs=[smem] + [vmem] * 5,
        out_specs=(hbm,) * 5,
        scratch_shapes=[v((4, 16, 1024), bf16), dma((5,))],
        compiler_params=pltpu.CompilerParams(vmem_limit_bytes=vmem_bytes),
    )(block_of_slot, *outs)


def solution(mesh):
    return jax.shard_map(
        local,
        mesh=mesh,
        in_specs=(
            P("fsdp", None, None, "tp"),
            P(),
            P("fsdp", "tp", None),
            P("fsdp", "tp", None),
            P("fsdp", "tp", None),
            P("fsdp", "tp", None),
            P("fsdp", "tp", None),
            P("fsdp", "tp", None),
        ),
        out_specs=(
            P(None, "fsdp", "tp"),
            P("fsdp", "tp", None),
            P("fsdp", "tp", None),
            P("fsdp", "tp", None),
            P("fsdp", "tp", None),
        ),
        check_vma=False,
    )
```

time: 94.1 us -> 82.9 us (0.88)
  local copies, waits for them, and re-layouts: 6.97 us -> 0 us
  Pallas kernels: 85.5 us -> 82.1 us
    unnamed x13 -> x0, local copies, waits for them, and re-layouts: 6.97 us -> none
    pallas_call x1 -> x2, Pallas kernels: 85.5 us -> 82.1 us  [the longest x1 78.7 us: local(): pl.pallas_call(kernel, name='step', out_shape=(jax.ShapeDtypeStruct((32,...]
where the time goes in v2:
time: 82.9 us; the launch traced here: 82.7 us
  Pallas kernels  82.1 us (99%)
    pallas_call x1, Pallas kernels, local(): pl.pallas_call(kernel, name='step', out_shape=(jax.ShapeDtypeStruct((32,...  78.7 us
    pallas_call x1, Pallas kernels, local(): pl.pallas_call(finish, name='finish', out_shape=(jax.ShapeDtypeStruct((4,...  3.35 us

profile of v2, /device:TPU:1, one launch (start us, length us, event | category | flops | bytes accessed | tf_op | source)
XLA Modules:
  0.0 82.7 jit_solution(17335165878066159207)
XLA Ops:
  0.6 78.7 %step.1 = (bf16[32,16,128]{2,1,0:T(8,128)(2,1)}, f32[2,64,512]{2,1,0:T(8,128)}, f32[2,64,512]{2,1,0:T(8,128)}, f32[2,64,512]{2,1,0:T(8,128)}, f32[2,64,512]{2,1,0:T(8,128)}) custom-call(s32[64]{0:T(128)} %bos.3, f32[8,256,1024]{2,1,0:T(8,128)} %bitcast.1, f32[2,64,512]{2,1,0:T(8,128)} %sl_h.1, f32[2,64,512]{2,1,0:T(8,128)} %sr_h.1, f32[2,64,512]{2,1,0:T(8,128)} %bl_h.1, ...), custom_call_target="tpu_custom_call" | custom-call | tf_op jit(solution)/shard_map/step/pallas_call | solution.py:494
  79.4 3.4 %finish.1 = (bf16[4,16,1024]{2,1,0:T(8,128)(2,1)}, f32[2,64,512]{2,1,0:T(8,128)}, f32[2,64,512]{2,1,0:T(8,128)}, f32[2,64,512]{2,1,0:T(8,128)}, f32[2,64,512]{2,1,0:T(8,128)}) custom-call(s32[64]{0:T(128)} %bos.3, bf16[32,16,128]{2,1,0:T(8,128)(2,1)} %get-tuple-element.10.rows, f32[2,64,512]{2,1,0:T(8,128)} %get-tuple-element.11.nl, ...), custom_call_target="tpu_custom_call" | custom-call | tf_op jit(solution)/shard_map/finish/pallas_call | solution.py:541

commit v3 on v2

--- a/solution.py
+++ b/solution.py
@@ -59,8 +59,8 @@
     bos, grad_h, sl_h, sr_h, bl_h, br_h, mo_h, se_h,
     a2r, nl, nr, nm, ns,
     g, sl, sr, bl, br, mo, se,
-    cs, cr, xq, xqr, xs, xr, zs, zr, za, gslab, ag, ah, lm, left, rmsg, rc, rct, gt, hb, tmp, bk, part, a2s,
-    loc, g_sem, out_sem, c_s, c_r, q_s, q_r, x_s, x_r, z_s, z_r, l_s, l_r, r_s, r_r, g_s, g_r, h_s, h_r, a_s, a_r,
+    cs, cr, xq, xqr, xs, xr, zs, zr, za, gslab, ag, ah, lm, left, rmsg, rc, rct, gt, hb, tmp, bk, part, pb, pbr, a2s,
+    loc, g_sem, out_sem, c_s, c_r, q_s, q_r, x_s, x_r, z_s, z_r, l_s, l_r, r_s, r_r, g_s, g_r, h_s, h_r, p_s, p_r, a_s, a_r,
 ):
     f = lax.axis_index("fsdp")
     t = lax.axis_index("tp")
@@ -101,9 +101,8 @@
     def _(d):
         pl.semaphore_signal(barrier, inc=1, device_id=((f + d) % 32, t), device_id_type=MESH)
 
-    @pl.loop(1, 8)
-    def _(d):
-        pl.semaphore_signal(barrier, inc=1, device_id=(f, (t + d) % 8), device_id_type=MESH)
+    for peer in [tdev(1 - zh, y)] + [tdev(zh, (y + d) % 4) for d in FAR]:
+        pl.semaphore_signal(barrier, inc=1, device_id=peer, device_id_type=MESH)
 
     def core_copy(s, dx):
         return remote(cs.at[s, dx], cr.at[s, dx], c_s.at[s, dx], c_r.at[s, dx], fdev(x, zl, 1 - c))
@@ -139,13 +138,16 @@
         for s in range(2)
     ]
     h_copies = [
-        tp_copies(lambda k, s=s: ah.at[s, k], lambda i, s=s: h_s.at[s, i], lambda i, s=s: h_r.at[s, i])
+        [
+            remote(ah.at[s, t], ah.at[s, t], h_s.at[s, d - 1], h_r.at[s, d - 1], tdev(zh, (y + d) % 4))
+            for d in FAR
+        ]
         for s in range(2)
     ]
-
-    def right_copy(d):
-        k = (t + d) % 8
-        return remote(rmsg.at[k], rc.at[t], r_s.at[d], r_r.at[d], (f, k))
+    p_copies = [remote(pb.at[s], pbr.at[s], p_s.at[s], p_r.at[s], tdev(1 - zh, y)) for s in range(2)]
+    right_copies = [
+        remote(rmsg.at[(y + d) % 4], rc.at[y], r_s.at[d - 1], r_r.at[d - 1], tdev(zh, (y + d) % 4)) for d in FAR
+    ]
 
     def a2a_copy(d):
         k = (f + d) % 32
@@ -164,7 +166,7 @@
         for cp in copies:
             cp.wait_send()
 
-    pl.semaphore_wait(barrier, 38)
+    pl.semaphore_wait(barrier, 35)
 
     def stacked(v):
         return jnp.concatenate([v[:, q * 128 : q * 128 + 128] for q in range(4)], axis=0)
@@ -177,6 +179,7 @@
         leaving["left", 0] = lambda: wait_sent(left_first)
 
     def send_right():
+        loads[1].wait()
         lanes = lane_iota(64)
         for u in range(4):
             a = br[0, :, u * 128 : u * 128 + 128]
@@ -184,20 +187,11 @@
             even, odd = jnp.where(lanes < 64, a, roll_half(b)), jnp.where(lanes < 64, roll_half(a), b)
             for k, v in ((2 * u, even), (2 * u + 1, odd)):
                 high, low = split(v)
-                rmsg[k, 0] = high
-                rmsg[k, 1] = low
-        rc[t] = rmsg[t]
-
-        @pl.loop(1, 8)
-        def _(d):
-            right_copy(d).start()
-
-        def sent():
-            @pl.loop(1, 8)
-            def _(d):
-                right_copy(d).wait_send()
-
-        leaving["right",] = sent
+                rmsg[k % 4, k // 4, 0] = high
+                rmsg[k % 4, k // 4, 1] = low
+        rc[y] = rmsg[y]
+        start(right_copies)
+        leaving["right", 0] = lambda: wait_sent(right_copies)
 
     def extract(slot):
         b = bos[slot]
@@ -304,28 +298,28 @@
 
     def half_product(a, store, s, half):
         k = pl.ds(pl.multiple_of(half * 256, 256), 256)
-        return dot3(a[:, k], store[s, 0, k, :], store[s, 1, k, :], PLAIN)
+        return dot3(a(k), store[s, 0, k, :], store[s, 1, k, :], PLAIN)
 
     def near_half(copies, messages, s, store, a):
-        for cp in copies[0][1:]:
+        for cp in copies:
             cp.wait_recv()
         unpack(lambda k: messages.at[s, k], s, store, zh)
-        part[s] = half_product(a, store, s, zh)
+        return half_product(a, store, s, zh)
 
     def far_half(copies, messages, s, store, a):
-        for cp in copies[1]:
+        for cp in copies:
             cp.wait_recv()
         unpack(lambda k: messages.at[s, k], s, store, 1 - zh)
-        return part[s] + half_product(a, store, s, 1 - zh)
+        return half_product(a, store, s, 1 - zh)
 
     def put(ref, dst, i, s):
         return pltpu.make_async_copy(ref.at[s], dst.at[s], out_sem.at[i, s])
 
     def rotate_near(s):
-        near_half(g_copies[s], ag, s, gt, br.at[s])
+        part[s] = near_half(g_copies[s][0][1:], ag, s, gt, lambda k: br[s, :, k])
 
     def rotate(s):
-        partial = far_half(g_copies[s], ag, s, gt, br.at[s])
+        partial = part[s] + far_half(g_copies[s][1], ag, s, gt, lambda k: br[s, :, k])
         rotated = dot3(partial, left[s, 0], left[s, 1], MINOR)
         new_moment = first_decay * mo[s] + (1.0 - first_decay) * rotated
         new_second = second_decay * se[s] + (1.0 - second_decay) * rotated * rotated
@@ -334,8 +328,8 @@
         direction = new_moment / (jnp.sqrt(new_second) + epsilon)
         half = dot3(direction, left[s, 0], left[s, 1], PLAIN)
         encode(stacked(half), ah.at[s, t])
-        start(h_copies[s][0])
-        leaving["h", s] = lambda: wait_sent(h_copies[s][0])
+        start(h_copies[s])
+        leaving["h", s] = lambda: wait_sent(h_copies[s])
         put(mo, nm, 0, s).start()
         put(se, ns, 1, s).start()
 
@@ -352,10 +346,20 @@
         put(sl, nl, 3, s).start()
 
     def back_near(s):
-        near_half(h_copies[s], ah, s, hb, rct.at[pl.ds(s * 64, 64)])
+        rows = pl.ds(s * 64, 64)
+        both = near_half(
+            h_copies[s], ah, s, hb, lambda k: jnp.concatenate([rct[1 - zh, rows, :], rct[zh, rows, :]], axis=0)
+        )
+        encode(stacked(both[0:64]), pb.at[s])
+        p_copies[s].start()
+        leaving["p", s] = lambda: p_copies[s].wait_send()
+        bk[rows, :] = both[64:128]
 
     def back(s):
-        bk[pl.ds(s * 64, 64), :] = far_half(h_copies[s], ah, s, hb, rct.at[pl.ds(s * 64, 64)])
+        p_copies[s].wait_recv()
+        other = decode(pbr.at[s])
+        for q in range(4):
+            bk[s * 64 : s * 64 + 64, q * 128 : q * 128 + 128] += other[q * 64 : q * 64 + 64]
 
     def grad_ready():
         @pl.loop(0, 8)
@@ -363,14 +367,13 @@
             grad_load(i).wait()
 
     def right_ready():
-        @pl.loop(1, 8)
-        def _(d):
-            right_copy(d).wait_recv()
-
-        rct[...] = jnp.concatenate([rc[k, 0].astype(f32) + rc[k, 1].astype(f32) for k in range(8)], axis=0).T
+        for cp in right_copies:
+            cp.wait_recv()
+        for h in range(2):
+            rct[h] = jnp.concatenate([rc[k, h, 0].astype(f32) + rc[k, h, 1].astype(f32) for k in range(4)], axis=0).T
 
     def left_ready():
-        for cp in loads[1:]:
+        for cp in loads[2:]:
             cp.wait()
         for cp in left_first[1:] + left_second:
             cp.wait_recv()
@@ -396,6 +399,7 @@
         lambda: core_part(0, 1),
         lambda: send_left(),
         lambda: relay_stage(0),
+        lambda: send_right(),
         lambda: core_part(0, 0),
         lambda: core_part(1, 2),
         lambda: near_stage(0, 0),
@@ -428,17 +432,14 @@
         lambda: g_stage(1),
         lambda: rotate(0),
         lambda: forward("g", 1, g_copies[1]),
-        lambda: send_right(),
         lambda: rotate_near(1),
+        lambda: right_ready(),
+        lambda: back_near(0),
         lambda: rotate(1),
-        lambda: forward("h", 0, h_copies[0]),
         lambda: statistics(0),
-        lambda: right_ready(),
-        lambda: forward("h", 1, h_copies[1]),
-        lambda: back_near(0),
+        lambda: back_near(1),
         lambda: back(0),
         lambda: statistics(1),
-        lambda: back_near(1),
         lambda: back(1),
         lambda: send_back(),
     ]
@@ -466,18 +467,16 @@
 
     upper = lane_iota(16) >= 64
 
-    @pl.loop(0, 16)
-    def _(k):
-        for u in range(2):
-            both = rows[2 * k + u].astype(f32)
-            turned = roll_half(both)
-            for j in range(2):
-                b = bos[4 * k + 2 * u + j]
-                half = b % 2
-                cols = pl.ds(pl.multiple_of(b % 16 // 2 * 128, 128), 128)
-                old = upd[b // 16, :, cols]
-                new = jnp.where((lane_iota(16) * 0 + half) == j, both, turned).astype(bf16)
-                upd[b // 16, :, cols] = jnp.where(upper == ((lane_iota(16) * 0 + half) == 1), new, old)
+    for k in range(32):
+        both = rows[k].astype(f32)
+        turned = roll_half(both)
+        for j in range(2):
+            b = bos[2 * k + j]
+            half = b & 1
+            cols = pl.ds(pl.multiple_of(((b & 15) >> 1) * 128, 128), 128)
+            old = upd[b >> 4, :, cols]
+            new = jnp.where((lane_iota(16) * 0 + half) == j, both, turned).astype(bf16)
+            upd[b >> 4, :, cols] = jnp.where(upper == ((lane_iota(16) * 0 + half) == 1), new, old)
 
     outs[4].start()
     for out in outs:
@@ -514,14 +513,16 @@
             v((2, 8, 272, 128), i16),
             v((8, 2, 272, 128), i16),
             v((2, 2, 512, 512), bf16),
-            v((8, 2, 64, 128), bf16),
-            v((8, 2, 64, 128), bf16),
-            v((128, 512), f32),
+            v((4, 2, 2, 64, 128), bf16),
+            v((4, 2, 2, 64, 128), bf16),
+            v((2, 128, 256), f32),
             v((2, 2, 512, 512), bf16),
             v((2, 2, 512, 512), bf16),
             v((128, 512), f32),
             v((128, 512), f32),
             v((2, 64, 512), f32),
+            v((2, 272, 128), i16),
+            v((2, 272, 128), i16),
             v((32, 16, 128), bf16),
             dma((6,)),
             dma((8,)),
@@ -530,8 +531,10 @@
             *[dma((2, 2, 4))] * 2,
             *[dma((2, 3))] * 2,
             *[dma((7,))] * 2,
-            *[dma((8,))] * 2,
-            *[dma((2, 7))] * 4,
+            *[dma((3,))] * 2,
+            *[dma((2, 7))] * 2,
+            *[dma((2, 3))] * 2,
+            *[dma((2,))] * 2,
             *[dma((32,))] * 2,
         ],
         compiler_params=pltpu.CompilerParams(

time: 82.9 us -> 79.2 us (0.955)
  Pallas kernels: 82.1 us -> 78.5 us
    pallas_call x1, Pallas kernels: 78.7 us -> 76.1 us  [local(): pl.pallas_call(kernel, name='step', out_shape=(jax.ShapeDtypeStruct((32,...]
    pallas_call x1, Pallas kernels: 3.35 us -> 2.42 us  [local(): pl.pallas_call(finish, name='finish', out_shape=(jax.ShapeDtypeStruct((4,...]
where the time goes in v3:
time: 79.2 us; the launch traced here: 79.1 us
  Pallas kernels  78.5 us (99%)
    pallas_call x1, Pallas kernels, local(): pl.pallas_call(kernel, name='step', out_shape=(jax.ShapeDtypeStruct((32,...  76.1 us
    pallas_call x1, Pallas kernels, local(): pl.pallas_call(finish, name='finish', out_shape=(jax.ShapeDtypeStruct((4,...  2.42 us

profile of v3, /device:TPU:1, one launch (start us, length us, event | category | flops | bytes accessed | tf_op | source)
XLA Modules:
  0.0 79.1 jit_solution(1925111302207640365)
XLA Ops:
  0.6 76.1 %step.1 = (bf16[32,16,128]{2,1,0:T(8,128)(2,1)}, f32[2,64,512]{2,1,0:T(8,128)}, f32[2,64,512]{2,1,0:T(8,128)}, f32[2,64,512]{2,1,0:T(8,128)}, f32[2,64,512]{2,1,0:T(8,128)}) custom-call(s32[64]{0:T(128)} %bos.3, f32[8,256,1024]{2,1,0:T(8,128)} %bitcast.1, f32[2,64,512]{2,1,0:T(8,128)} %sl_h.1, f32[2,64,512]{2,1,0:T(8,128)} %sr_h.1, f32[2,64,512]{2,1,0:T(8,128)} %bl_h.1, ...), custom_call_target="tpu_custom_call" | custom-call | tf_op jit(solution)/shard_map/step/pallas_call | solution.py:493
  76.7 2.4 %finish.1 = (bf16[4,16,1024]{2,1,0:T(8,128)(2,1)}, f32[2,64,512]{2,1,0:T(8,128)}, f32[2,64,512]{2,1,0:T(8,128)}, f32[2,64,512]{2,1,0:T(8,128)}, f32[2,64,512]{2,1,0:T(8,128)}) custom-call(s32[64]{0:T(128)} %bos.3, bf16[32,16,128]{2,1,0:T(8,128)(2,1)} %get-tuple-element.10.rows, f32[2,64,512]{2,1,0:T(8,128)} %get-tuple-element.11.nl, ...), custom_call_target="tpu_custom_call" | custom-call | tf_op jit(solution)/shard_map/finish/pallas_call | solution.py:544

commit v4 on v3

--- a/solution.py
+++ b/solution.py
@@ -104,8 +104,10 @@
     for peer in [tdev(1 - zh, y)] + [tdev(zh, (y + d) % 4) for d in FAR]:
         pl.semaphore_signal(barrier, inc=1, device_id=peer, device_id_type=MESH)
 
-    def core_copy(s, dx):
-        return remote(cs.at[s, dx], cr.at[s, dx], c_s.at[s, dx], c_r.at[s, dx], fdev(x, zl, 1 - c))
+    def core_copy(s, dx, z):
+        return remote(
+            cs.at[s, dx, z], cr.at[s, dx, z], c_s.at[s, dx, z], c_r.at[s, dx, z], fdev(x, zl, 1 - c)
+        )
 
     def relay_copy(s, i):
         return remote(
@@ -207,18 +209,24 @@
 
     def core_part(s, dx):
         @pl.loop(0, 4)
-        def _(z):
+        def _(j):
+            z = (zl + 1 + j // 2 + 2 * (j % 2)) % 4
             cs[s, dx, z] = extract(slot_of(s, dx, z, 1 - c))
-
-        core_copy(s, dx).start()
-        leaving["core", s, dx] = lambda: core_copy(s, dx).wait_send()
+            core_copy(s, dx, z).start()
+
+        def sent():
+            @pl.loop(0, 4)
+            def _(z):
+                core_copy(s, dx, z).wait_send()
+
+        leaving["core", s, dx] = sent
 
     def pair_sum(s, dx, z):
-        return extract(slot_of(s, dx, z, c)) + cr[s, dx, z]
+        own = extract(slot_of(s, dx, z, c))
+        core_copy(s, dx, z).wait_recv()
+        return own + cr[s, dx, z]
 
     def relay_stage(s):
-        core_copy(s, 2).wait_recv()
-
         @pl.loop(0, 4)
         def _(j):
             i = j // 2 + 2 * (j % 2)
@@ -234,8 +242,6 @@
 
     def near_stage(s, j):
         for way in (1, 0):
-            if j == 0:
-                core_copy(s, 1 + 2 * way).wait_recv()
             i = j + 2 - 2 * way
             encode(pair_sum(s, 1 + 2 * way, (zl + 1 + i) % 4), xs.at[s, way, i])
             x_copy(s, way, i).start()
@@ -258,8 +264,6 @@
         return total
 
     def z_send(s, dz):
-        if dz == 1:
-            core_copy(s, 0).wait_recv()
         encode(x_sum(s, dz - 1), zs.at[s, dz - 1])
         z_copy(s, dz).start()
         leaving["z", s, dz] = lambda: z_copy(s, dz).wait_send()
@@ -527,7 +531,8 @@
             dma((6,)),
             dma((8,)),
             dma((4, 2)),
-            *[dma((2, 4))] * 4,
+            *[dma((2, 4, 4))] * 2,
+            *[dma((2, 4))] * 2,
             *[dma((2, 2, 4))] * 2,
             *[dma((2, 3))] * 2,
             *[dma((7,))] * 2,

time: 79.2 us -> 76.6 us (0.967)
  Pallas kernels: 78.5 us -> 75.9 us
    pallas_call x1, Pallas kernels: 76.1 us -> 73.4 us  [local(): pl.pallas_call(kernel, name='step', out_shape=(jax.ShapeDtypeStruct((32,...]
where the time goes in v4:
time: 76.6 us; the launch traced here: 76.5 us
  Pallas kernels  75.9 us (99%)
    pallas_call x1, Pallas kernels, local(): pl.pallas_call(kernel, name='step', out_shape=(jax.ShapeDtypeStruct((32,...  73.4 us
    pallas_call x1, Pallas kernels, local(): pl.pallas_call(finish, name='finish', out_shape=(jax.ShapeDtypeStruct((4,...  2.43 us

profile of v4, /device:TPU:1, one launch (start us, length us, event | category | flops | bytes accessed | tf_op | source)
XLA Modules:
  0.0 76.5 jit_solution(2323641261969004205)
XLA Ops:
  0.6 73.4 %step.1 = (bf16[32,16,128]{2,1,0:T(8,128)(2,1)}, f32[2,64,512]{2,1,0:T(8,128)}, f32[2,64,512]{2,1,0:T(8,128)}, f32[2,64,512]{2,1,0:T(8,128)}, f32[2,64,512]{2,1,0:T(8,128)}) custom-call(s32[64]{0:T(128)} %bos.3, f32[8,256,1024]{2,1,0:T(8,128)} %bitcast.1, f32[2,64,512]{2,1,0:T(8,128)} %sl_h.1, f32[2,64,512]{2,1,0:T(8,128)} %sr_h.1, f32[2,64,512]{2,1,0:T(8,128)} %bl_h.1, ...), custom_call_target="tpu_custom_call" | custom-call | tf_op jit(solution)/shard_map/step/pallas_call | solution.py:497
  74.1 2.4 %finish.1 = (bf16[4,16,1024]{2,1,0:T(8,128)(2,1)}, f32[2,64,512]{2,1,0:T(8,128)}, f32[2,64,512]{2,1,0:T(8,128)}, f32[2,64,512]{2,1,0:T(8,128)}, f32[2,64,512]{2,1,0:T(8,128)}) custom-call(s32[64]{0:T(128)} %bos.3, bf16[32,16,128]{2,1,0:T(8,128)(2,1)} %get-tuple-element.10.rows, f32[2,64,512]{2,1,0:T(8,128)} %get-tuple-element.11.nl, ...), custom_call_target="tpu_custom_call" | custom-call | tf_op jit(solution)/shard_map/finish/pallas_call | solution.py:549

commit v5 on v4

--- a/solution.py
+++ b/solution.py
@@ -37,7 +37,9 @@
 
 def dot3(a, bh, bl, dims):
     ah, al = split(a)
-    return dot(ah, bh, dims) + (dot(ah, bl, dims) + dot(al, bh, dims))
+    n = a.shape[0]
+    both = dot(jnp.concatenate([ah, al], axis=0), bh, dims)
+    return both[:n] + (dot(ah, bl, dims) + both[n:])
 
 
 def encode(v, ref):
@@ -59,7 +61,7 @@
     bos, grad_h, sl_h, sr_h, bl_h, br_h, mo_h, se_h,
     a2r, nl, nr, nm, ns,
     g, sl, sr, bl, br, mo, se,
-    cs, cr, xq, xqr, xs, xr, zs, zr, za, gslab, ag, ah, lm, left, rmsg, rc, rct, gt, hb, tmp, bk, part, pb, pbr, a2s,
+    cs, cr, xq, xqr, xs, xr, zs, zr, za, gslab, ag, ah, lm, left, left_t, rmsg, rc, rct, gt, hb, tmp, bk, part, pb, pbr, a2s,
     loc, g_sem, out_sem, c_s, c_r, q_s, q_r, x_s, x_r, z_s, z_r, l_s, l_r, r_s, r_r, g_s, g_r, h_s, h_r, p_s, p_r, a_s, a_r,
 ):
     f = lax.axis_index("fsdp")
@@ -324,7 +326,7 @@
 
     def rotate(s):
         partial = part[s] + far_half(g_copies[s][1], ag, s, gt, lambda k: br[s, :, k])
-        rotated = dot3(partial, left[s, 0], left[s, 1], MINOR)
+        rotated = dot3(partial, left_t[s, 0], left_t[s, 1], PLAIN)
         new_moment = first_decay * mo[s] + (1.0 - first_decay) * rotated
         new_second = second_decay * se[s] + (1.0 - second_decay) * rotated * rotated
         mo[s] = new_moment
@@ -384,6 +386,8 @@
         for s in range(2):
             unpack(lambda k: lm.at[k, s], s, left, 0)
             unpack(lambda k: lm.at[k, s], s, left, 1)
+            for h in range(2):
+                left_t[s, h] = left[s, h].T
 
     def send_back():
         rows = bk[...].T.astype(bf16)
@@ -517,6 +521,7 @@
             v((2, 8, 272, 128), i16),
             v((8, 2, 272, 128), i16),
             v((2, 2, 512, 512), bf16),
+            v((2, 2, 512, 512), bf16),
             v((4, 2, 2, 64, 128), bf16),
             v((4, 2, 2, 64, 128), bf16),
             v((2, 128, 256), f32),

time: 76.6 us -> 77.1 us (level)
  no operation moved by 1% of the time
where the time goes in v5:
time: 77.1 us; the launch traced here: 77 us
  Pallas kernels  76.3 us (99%)
    pallas_call x1, Pallas kernels, local(): pl.pallas_call(kernel, name='step', out_shape=(jax.ShapeDtypeStruct((32,...  73.9 us
    pallas_call x1, Pallas kernels, local(): pl.pallas_call(finish, name='finish', out_shape=(jax.ShapeDtypeStruct((4,...  2.42 us

profile of v5, /device:TPU:1, one launch (start us, length us, event | category | flops | bytes accessed | tf_op | source)
XLA Modules:
  0.0 77.0 jit_solution(8100672357144889016)
XLA Ops:
  0.6 73.9 %step.1 = (bf16[32,16,128]{2,1,0:T(8,128)(2,1)}, f32[2,64,512]{2,1,0:T(8,128)}, f32[2,64,512]{2,1,0:T(8,128)}, f32[2,64,512]{2,1,0:T(8,128)}, f32[2,64,512]{2,1,0:T(8,128)}) custom-call(s32[64]{0:T(128)} %bos.3, f32[8,256,1024]{2,1,0:T(8,128)} %bitcast.1, f32[2,64,512]{2,1,0:T(8,128)} %sl_h.1, f32[2,64,512]{2,1,0:T(8,128)} %sr_h.1, f32[2,64,512]{2,1,0:T(8,128)} %bl_h.1, ...), custom_call_target="tpu_custom_call" | custom-call | tf_op jit(solution)/shard_map/step/pallas_call | solution.py:501
  74.6 2.4 %finish.1 = (bf16[4,16,1024]{2,1,0:T(8,128)(2,1)}, f32[2,64,512]{2,1,0:T(8,128)}, f32[2,64,512]{2,1,0:T(8,128)}, f32[2,64,512]{2,1,0:T(8,128)}, f32[2,64,512]{2,1,0:T(8,128)}) custom-call(s32[64]{0:T(128)} %bos.3, bf16[32,16,128]{2,1,0:T(8,128)(2,1)} %get-tuple-element.10.rows, f32[2,64,512]{2,1,0:T(8,128)} %get-tuple-element.11.nl, ...), custom_call_target="tpu_custom_call" | custom-call | tf_op jit(solution)/shard_map/finish/pallas_call | solution.py:554
